TPU v7x, 32 devices: a whole 2x2x4 slice. The times are simulated.
32 devices in a mesh: groups: 2 (over x), goal: 16 (over z, y, core).
Axes of the slice: x: 2, y: 2, z: 4, core: 2. Of those that a mesh axis runs over, the one named last changes fastest.
Arguments:
- queries: bfloat16 [128, 64, 4096], P(('groups', 'goal')), parts along dimension 0, may hold values from -8 to 8
- goal_keys: bfloat16 [32, 256, 4096], P(('groups', 'goal')), parts along dimension 0, may hold values from -8 to 8
- goal_values: bfloat16 [32, 256, 4096], P(('groups', 'goal')), parts along dimension 0, may hold values from -6 to 6
- out_weight: bfloat16 [4096, 2048], P('goal'), may hold values from -0.5 to 0.5
- tactic_goal: int32 [128, 1], P(('groups', 'goal')), parts along dimension 0, may hold values from 0 to 15
- tactic_len: int32 [128], P(('groups', 'goal')), parts along dimension 0, may hold values from 1 to 64
Outputs:
- projected: bfloat16 [128, 64, 2048], P(('groups', 'goal')), parts along dimension 0
There are 2 independent parts, one for each index of `groups`. A program takes and returns all parts, laid end to end along the dimension named above; an argument that names none is the same for every part. Nothing has to cross between parts.
Inputs may be any that keep to these rules, and one draw needn't show every extreme that they name: `tactic_goal`: every goal is read by at least one tactic; tactics per goal are uneven. `tactic_len`: the live positions of a tactic are its leading ones.
All inputs are finite; a program needn't handle non-finite values.
Results may differ from a plain program's by a relative error of at most 0.01.
Values may be sent and summed in bfloat16 or wider, within the bound.
A program may use at most 192 MiB of HBM per device.

v0:
```python
import math
import jax
import jax.numpy as jnp
from jax import lax
from jax.sharding import PartitionSpec as P

DH = 64


def attend_block(query_block, keys_heads, values_heads, block_ids):
    tact_count = query_block.shape[0]
    row_count = query_block.shape[1]
    width_local = query_block.shape[2]
    head_count = width_local // DH
    keys_tact = jnp.take(keys_heads, block_ids, axis=0).reshape(tact_count, -1, head_count, DH)
    vals_tact = jnp.take(values_heads, block_ids, axis=0).reshape(tact_count, -1, head_count, DH)
    query_four = query_block.reshape(tact_count, row_count, head_count, DH)
    scores = jnp.einsum(
        "tihd,tjhd->thij", query_four, keys_tact, preferred_element_type=jnp.float32
    )
    biggest = jnp.max(scores, axis=-1, keepdims=True)
    powers = jnp.exp(scores - biggest)
    weights = (powers / jnp.sum(powers, axis=-1, keepdims=True)).astype(jnp.bfloat16)
    attended = jnp.einsum("thij,tjhd->tihd", weights, vals_tact, preferred_element_type=jnp.float32)
    return attended.reshape(tact_count, row_count, width_local).astype(jnp.bfloat16)


def attend(query_piece, keys_heads, values_heads, goal_ids):
    tact_count = query_piece.shape[0]
    row_count = query_piece.shape[1]
    width_local = query_piece.shape[2]
    block_size = math.gcd(tact_count, 64)
    block_count = tact_count // block_size
    query_blocks = query_piece.reshape(block_count, block_size, row_count, width_local)
    id_blocks = goal_ids.reshape(block_count, block_size)

    def one_block(operands):
        return attend_block(operands[0], keys_heads, values_heads, operands[1])

    results = lax.map(one_block, (query_blocks, id_blocks))
    return results.reshape(tact_count, row_count, width_local)


def shards(queries, goal_keys, goal_values, out_weight, tactic_goal, tactic_len):
    goal_ids = lax.all_gather(tactic_goal[:, 0], "goal", axis=0, tiled=True)
    keys_heads, values_heads = (
        lax.all_to_all(goal_keys, "goal", split_axis=2, concat_axis=0, tiled=True),
        lax.all_to_all(goal_values, "goal", split_axis=2, concat_axis=0, tiled=True),
    )
    query_heads = lax.all_to_all(queries, "goal", split_axis=2, concat_axis=0, tiled=True)
    attended = attend(query_heads, keys_heads, values_heads, goal_ids)
    merged = lax.all_to_all(attended, "goal", split_axis=0, concat_axis=2, tiled=True)
    live_rows = jnp.arange(merged.shape[1])[None, :] < tactic_len[:, None]
    context = jnp.where(live_rows[:, :, None], merged, jnp.zeros_like(merged))
    tact_local = context.shape[0]
    row_count = context.shape[1]
    flat = context.reshape(tact_local * row_count, context.shape[2])
    projected = jnp.dot(
        flat,
        lax.all_gather(out_weight, "goal", axis=0, tiled=True),
        preferred_element_type=jnp.float32,
    )
    return projected.astype(jnp.bfloat16).reshape(tact_local, row_count, out_weight.shape[1])


def solution(mesh):
    return jax.shard_map(
        shards,
        mesh=mesh,
        in_specs=(
            P(("groups", "goal"), None, None),
            P(("groups", "goal"), None, None),
            P(("groups", "goal"), None, None),
            P("goal", None),
            P(("groups", "goal"), None),
            P(("groups", "goal")),
        ),
        out_specs=P(("groups", "goal"), None, None),
        check_vma=False,
    )
```

profile of v0, /device:TPU:13, one launch (start us, length us, event | category | flops | bytes accessed | tf_op | source)
XLA Modules:
  0.0 509.1 jit_solution(2314349538631211243)
XLA Ops:
  6.5 0.7 all-gather.3.cloned.1.call-update
  7.3 10.1 %copy.23 = bf16[1,256,4096]{1,0,2:T(2,128)(2,1)} copy(bf16[1,256,4096]{2,1,0:T(8,128)(2,1)} %param.10) | data formatting | bytes 4194304 | tf_op args[2]
  17.3 0.5 broadcast.32
  17.8 21.7 %reduce.1 = bf16[4096,256]{1,0:T(8,128)(2,1)S(1)} reduce(bf16[4096,1,256]{2,1,0:T(2,128)(2,1)} %bitcast.58, bf16[]{:T(256)} %broadcast.32), dimensions={1}, to_apply=%bitcast.44.reduce_sub_computation | reduce | bytes 4194306
  39.5 2.1 reshape.91
  41.6 6.6 %all-to-all-start = ((bf16[16,2,32768]{2,1,0:T(2,128)(2,1)}), bf16[16,2,32768]{2,1,0:T(2,128)(2,1)S(1)}, u32[]{:S(2)}, u32[]{:S(2)}) async-start(bf16[16,2,32768]{2,1,0:T(2,128)(2,1)} %reshape.91), calls=%async_computation | async-start | bytes 4194304 | tf_op jit(solution)/shard_map/all_to_all | solution.py:48
  48.1 10.1 %copy.26 = bf16[1,256,4096]{1,0,2:T(2,128)(2,1)} copy(bf16[1,256,4096]{2,1,0:T(8,128)(2,1)} %param.9) | data formatting | bytes 4194304 | tf_op args[1]
  58.2 23.0 %reduce = bf16[4096,256]{1,0:T(8,128)(2,1)} reduce(bf16[4096,1,256]{2,1,0:T(2,128)(2,1)} %bitcast.59, bf16[]{:T(256)} %broadcast.32), dimensions={1}, to_apply=%bitcast.46.reduce_sub_computation | reduce | bytes 4194306
  81.1 4.0 reshape.93
  85.1 58.2 %all-to-all-done = bf16[16,2,32768]{2,1,0:T(2,128)(2,1)S(1)} async-done(((bf16[16,2,32768]{2,1,0:T(2,128)(2,1)}), bf16[16,2,32768]{2,1,0:T(2,128)(2,1)S(1)}, u32[]{:S(2)}, u32[]{:S(2)}) %all-to-all-start) | async-done | bytes 2097184 | tf_op jit(solution)/shard_map/all_to_all | solution.py:48
  143.3 4.3 all-to-all-start.1
  147.7 0.0 copy-start.2
  147.7 0.0 copy-start
  147.7 7.0 %copy.29 = bf16[4,64,4096]{1,0,2:T(4,128)(2,1)} copy(bf16[4,64,4096]{2,1,0:T(8,128)(2,1)} %param.8) | data formatting | bytes 4194304 | tf_op args[0]
  154.7 7.5 %reshape.95 = bf16[16,2,32768]{2,1,0:T(2,128)(2,1)} reshape(bf16[4096,4,64]{2,1,0:T(4,128)(2,1)} %bitcast.63) | data formatting | bytes 4194304
  162.3 52.0 %all-to-all-done.1 = bf16[16,2,32768]{2,1,0:T(2,128)(2,1)} async-done(((bf16[16,2,32768]{2,1,0:T(2,128)(2,1)}), bf16[16,2,32768]{2,1,0:T(2,128)(2,1)}, u32[]{:S(2)}, u32[]{:S(2)}) %all-to-all-start.1) | async-done | bytes 2097184 | tf_op jit(solution)/shard_map/all_to_all | solution.py:47
  214.3 4.7 all-to-all-start.2
  219.0 0.0 copy-done.2
  219.0 0.6 dynamic-slice.1
  220.3 0.1 bitcast_dynamic-update-slice_fusion
  220.4 44.1 %all-reduce = s32[64]{0:T(128)S(1)} all-reduce(s32[64]{0:T(128)S(1)} %bitcast_dynamic-update-slice_fusion), channel_id=2, replica_groups=mesh['groups'=2,'goal'=16] {'goal'}, use_global_device_ids=true, to_apply=%add | all-reduce | flops 64 | bytes 512 | tf_op jit(solution)/shard_map/all_gather | solution.py:45
  264.5 6.8 %reshape.92 = bf16[4096,1,256]{2,1,0:T(2,128)(2,1)} reshape(bf16[16,2,32768]{2,1,0:T(2,128)(2,1)S(1)} %all-to-all-done) | data formatting | bytes 4194304
  271.3 3.9 copy.34
  275.1 2.8 copy.24
  278.0 10.5 %reshape.94 = bf16[4096,1,256]{2,1,0:T(2,128)(2,1)} reshape(bf16[16,2,32768]{2,1,0:T(2,128)(2,1)} %all-to-all-done.1) | data formatting | bytes 4194304
  288.5 3.9 copy.35
  292.4 3.9 copy.27
  296.3 5.5 %gather_fusion = bf16[64,256,256]{2,1,0:T(8,128)(2,1)} fusion(bf16[16,256,256]{2,1,0:T(8,128)(2,1)S(1)} %bitcast.56, s32[1024]{0:T(1024)S(1)} %pad_clamp_fusion), kind=kCustom, calls=%fused_computation.clone | custom fusion | bytes 16777472 | tf_op jit(solution)/shard_map/while/body/eval_jaxpr/jit(_take)/gather | solution.py:16
  301.8 7.1 %gather_fusion.1 = bf16[64,256,256]{2,1,0:T(8,128)(2,1)} fusion(bf16[16,256,256]{2,1,0:T(8,128)(2,1)} %bitcast.57, s32[1024]{0:T(1024)S(1)} %pad_clamp_fusion), kind=kCustom, calls=%fused_computation.1.clone | custom fusion | bytes 16777472 | tf_op jit(solution)/shard_map/while/body/eval_jaxpr/jit(_take)/gather | solution.py:15
  308.9 11.6 %broadcast_select_fusion = (bf16[64,256,256]{2,1,0:T(8,128)(2,1)}, bf16[64,256,256]{2,1,0:T(8,128)(2,1)}) fusion(bf16[64,256,256]{2,1,0:T(8,128)(2,1)} %gather_fusion.1, pred[64]{0:T(512)(128)(4,1)S(1)} %compare_and_fusion, bf16[64,256,256]{2,1,0:T(8,128)(2,1)} %gather_fusion), kind=kLoop, calls=%fused_computation.9 | loop fusion | flops 8388608 | bytes 33554496 | tf_op jit(solution)/shard_map/while/body/eval_jaxpr/jit(_take)/select_n | solution.py:15
  320.5 11.9 %copy.28 = bf16[64,256,256]{1,2,0:T(8,128)(2,1)} copy(bf16[64,256,256]{2,1,0:T(8,128)(2,1)} %get-tuple-element.16) | data formatting | bytes 16777216 | tf_op jit(solution)/shard_map/while/body/eval_jaxpr/jit(_take)/select_n | solution.py:15
  332.4 0.0 all-to-all-done.2
  332.4 7.5 %reshape.96 = bf16[4096,4,64]{2,1,0:T(4,128)(2,1)} reshape(bf16[16,2,32768]{2,1,0:T(2,128)(2,1)} %all-to-all-done.2) | data formatting | bytes 4194304
  339.9 5.4 %copy.30 = bf16[4,64,16,256]{3,1,0,2:T(8,128)(2,1)S(1)} copy(bf16[4,64,16,256]{1,0,3,2:T(4,128)(2,1)} %bitcast.62) | data formatting | bytes 4194304 | tf_op jit(solution)/shard_map/all_to_all | solution.py:50
  345.2 3.3 reshape.60
  348.5 11.9 %copy.25 = bf16[64,256,256]{1,2,0:T(8,128)(2,1)} copy(bf16[64,256,256]{2,1,0:T(8,128)(2,1)} %get-tuple-element.17) | data formatting | bytes 16777216 | tf_op jit(solution)/shard_map/while/body/eval_jaxpr/jit(_take)/select_n | solution.py:16
  360.4 12.7 %fusion.6 = f32[64,4,256,64]{2,3,1,0:T(8,128)} fusion(bf16[64,256,4,64]{1,3,2,0:T(8,128)(2,1)} %bitcast.55, bf16[64,64,4,64]{3,2,1,0:T(4,128)(2,1)} %reshape.60), kind=kOutput, calls=%fused_computation.11 | convolution fusion | flops 536870912 | bytes 27262976 | tf_op jit(solution)/shard_map/while/body/eval_jaxpr/tihd,tjhd->thij/dot_general | solution.py:18
  373.1 14.6 %fusion.18 = f32[64,4,64]{2,1,0:T(4,128)S(1)} fusion(f32[64,4,256,64]{2,3,1,0:T(8,128)} %fusion.6), kind=kOutput, calls=%fused_computation.25 | output fusion | flops 8388863 | bytes 16842752 | tf_op jit(solution)/shard_map/while/body/eval_jaxpr/sub | solution.py:22
  387.7 43.3 %fusion.8 = bf16[64,4,64,64]{3,2,1,0:T(8,128)(2,1)} fusion(bf16[64,256,4,64]{1,3,2,0:T(8,128)(2,1)} %bitcast.67, f32[64,4,64]{2,1,0:T(4,128)S(1)} %fusion.18, f32[64,4,256,64]{2,3,1,0:T(8,128)} %fusion.6), kind=kOutput, calls=%fused_computation.13 | convolution fusion | flops 550519040 | bytes 27328512 | tf_op jit(solution)/shard_map/while/body/eval_jaxpr/thij,tjhd->tihd/dot_general | solution.py:24
  431.1 4.8 copy.32
  435.9 7.5 %all-to-all-start.3 = ((bf16[64,64,256]{2,1,0:T(8,128)(2,1)}), bf16[64,64,256]{2,1,0:T(8,128)(2,1)S(1)}, u32[]{:S(2)}, u32[]{:S(2)}) async-start(bf16[64,64,256]{2,1,0:T(8,128)(2,1)} %copy.32), calls=%async_computation.3 | async-start | bytes 4194304 | tf_op jit(solution)/shard_map/all_to_all | solution.py:52
  443.4 0.1 iota_compare_fusion
  443.5 0.1 lt.30
  443.6 47.3 %all-to-all-done.3 = bf16[64,64,256]{2,1,0:T(8,128)(2,1)S(1)} async-done(((bf16[64,64,256]{2,1,0:T(8,128)(2,1)}), bf16[64,64,256]{2,1,0:T(8,128)(2,1)S(1)}, u32[]{:S(2)}, u32[]{:S(2)}) %all-to-all-start.3) | async-done | bytes 2097184 | tf_op jit(solution)/shard_map/all_to_all | solution.py:52
  490.8 1.2 copy.33
  492.0 0.9 copy.36
  492.9 0.0 all-gather.3.cloned.1.call-done
  493.0 9.3 %convolution_convert_fusion = bf16[256,2048]{1,0:T(8,128)(2,1)} fusion(bf16[4096,2048]{1,0:T(8,128)(2,1)} %all-gather.3.cloned.1.call-done, bf16[256,4096]{1,0:T(8,128)(2,1)S(1)} %bitcast.71, pred[256]{0:T(512)(128)(4,1)S(1)} %lt.30), kind=kOutput, calls=%fused_computation.14 | convolution fusion | flops 4296540160 | bytes 19923200 | tf_op jit(solution)/shard_map/dot_general | solution.py:58
  (8 shorter events, 0.0 us)
Async XLA Ops:
  6.5 486.4 %all-gather.3.cloned.1.call-start = ((), (), s32[]{:S(2)}) async-start(), calls=%async_computation.4 | async-start | bytes 17825792 | tf_op jit(solution)/shard_map/all_gather | solution.py:60
  41.6 101.8 %all-to-all-start = ((bf16[16,2,32768]{2,1,0:T(2,128)(2,1)}), bf16[16,2,32768]{2,1,0:T(2,128)(2,1)S(1)}, u32[]{:S(2)}, u32[]{:S(2)}) async-start(bf16[16,2,32768]{2,1,0:T(2,128)(2,1)} %reshape.91), calls=%async_computation | async-start | bytes 4194304 | tf_op jit(solution)/shard_map/all_to_all | solution.py:48
  143.3 71.0 %all-to-all-start.1 = ((bf16[16,2,32768]{2,1,0:T(2,128)(2,1)}), bf16[16,2,32768]{2,1,0:T(2,128)(2,1)}, u32[]{:S(2)}, u32[]{:S(2)}) async-start(bf16[16,2,32768]{2,1,0:T(2,128)(2,1)} %reshape.93), calls=%async_computation.1 | async-start | bytes 4194304 | tf_op jit(solution)/shard_map/all_to_all | solution.py:47
  147.7 71.4 %copy-start.2 = (u32[32]{0:T(128)S(1)}, u32[32]{0:T(128)}, u32[]{:S(2)}) copy-start(u32[32]{0:T(128)} %constant.37) | copy-start | bytes 388
  147.7 72.6 %copy-start = (s32[4,1]{0,1:T(1,128)S(1)}, s32[4,1]{0,1:T(1,128)}, u32[]{:S(2)}) copy-start(s32[4,1]{0,1:T(1,128)} %param.12) | copy-start | bytes 52
  214.3 118.2 %all-to-all-start.2 = ((bf16[16,2,32768]{2,1,0:T(2,128)(2,1)}), bf16[16,2,32768]{2,1,0:T(2,128)(2,1)}, u32[]{:S(2)}, u32[]{:S(2)}) async-start(bf16[16,2,32768]{2,1,0:T(2,128)(2,1)} %reshape.95), calls=%async_computation.2 | async-start | bytes 4194304 | tf_op jit(solution)/shard_map/all_to_all | solution.py:50
  431.1 12.3 %copy-start.1 = (s32[4]{0:T(128)S(1)}, s32[4]{0:T(128)}, u32[]{:S(2)}) copy-start(s32[4]{0:T(128)} %param.13) | copy-start | bytes 52
  435.9 54.9 %all-to-all-start.3 = ((bf16[64,64,256]{2,1,0:T(8,128)(2,1)}), bf16[64,64,256]{2,1,0:T(8,128)(2,1)S(1)}, u32[]{:S(2)}, u32[]{:S(2)}) async-start(bf16[64,64,256]{2,1,0:T(8,128)(2,1)} %copy.32), calls=%async_computation.3 | async-start | bytes 4194304 | tf_op jit(solution)/shard_map/all_to_all | solution.py:52
Sparse Core Ops, SparseCore 0:
  9.5 193.1 all-gather.2
where the time goes:
time: 512 us; the launch traced here: 509 us
  waiting for transfers between devices  158 us (31%)
  local copies, waits for them, and re-layouts  133 us (26%)
  other arithmetic  70.9 us (14%)
  matrix products  65.3 us (13%)
  blocking collectives  44.1 us (9%)
  starting transfers between devices  23.2 us (5%)
  between operations  14.2 us (3%)
    unnamed x22, local copies, waits for them, and re-layouts  75.4 us
    all_to_all x1, waiting for transfers between devices, shards(): lax.all_to_all(goal_values, 'goal', split_axis=2, concat_axis=0, tiled=True)  58.2 us
    all_to_all x1, waiting for transfers between devices, shards(): lax.all_to_all(goal_keys, 'goal', split_axis=2, concat_axis=0, tiled=True)  52 us
    all_to_all x1, waiting for transfers between devices, shards(): lax.all_to_all(attended, 'goal', split_axis=0, concat_axis=2, tiled=True)  47.3 us
    unnamed x2, other arithmetic  44.6 us
    all_gather x1, blocking collectives, shards(): goal_ids = lax.all_gather(tactic_goal[:, 0], 'goal', axis=0, tiled=True)  44.1 us
    dot_general x1, matrix products, attend_block(): jnp.einsum('thij,tjhd->tihd', weights, vals_tact, preferred_element_type=...  43.3 us
    sub x1, other arithmetic, attend_block(): powers = jnp.exp(scores - biggest)  14.6 us
  transfers between devices with their start and end apart: 5, of which 3 were waited for; matrix products, arithmetic and copies ran while one was open for 51% of the time, Pallas kernels for 0%

commit v1 on v0

--- a/solution.py
+++ b/solution.py
@@ -5,6 +5,18 @@
 from jax.sharding import PartitionSpec as P
 
 DH = 64
+
+
+def sent_to_each(value, axis, split, join):
+    ways, here = (lax.axis_size(axis), lax.axis_index(axis))
+    width = value.shape[split] // ways
+    turned = jnp.roll(value, -here * width, axis=split)
+    got = [lax.slice_in_dim(turned, 0, width, axis=split)]
+    for far in range(1, ways):
+        sent = lax.slice_in_dim(turned, far * width, (far + 1) * width, axis=split)
+        got.append(lax.ppermute(sent, axis, [(d, (d + far) % ways) for d in range(ways)]))
+    line = jnp.concatenate(got[::-1], axis=join)
+    return jnp.roll(line, (here + 1) * got[0].shape[join], axis=join)
 
 
 def attend_block(query_block, keys_heads, values_heads, block_ids):
@@ -44,7 +56,7 @@
 def shards(queries, goal_keys, goal_values, out_weight, tactic_goal, tactic_len):
     goal_ids = lax.all_gather(tactic_goal[:, 0], "goal", axis=0, tiled=True)
     keys_heads, values_heads = (
-        lax.all_to_all(goal_keys, "goal", split_axis=2, concat_axis=0, tiled=True),
+        sent_to_each(goal_keys, "goal", 2, 0),
         lax.all_to_all(goal_values, "goal", split_axis=2, concat_axis=0, tiled=True),
     )
     query_heads = lax.all_to_all(queries, "goal", split_axis=2, concat_axis=0, tiled=True)

time: 512 us -> 490 us (0.957)
  waiting for transfers between devices: 158 us -> 55.7 us
  starting transfers between devices: 23.2 us -> 81.2 us
  blocking collectives: 44.1 us -> 87.6 us
  other arithmetic: 70.9 us -> 50.5 us
    all_to_all x1, waiting for transfers between devices: 58.2 us -> 0.01 us  [shards(): lax.all_to_all(goal_values, 'goal', split_axis=2, concat_axis=0, tiled=True)]
    ppermute x0 -> x15, starting transfers between devices: none -> 55.8 us  [sent_to_each(): lax.ppermute(sent, axis, [(d, (d + far) % ways) for d in range(ways)])]
    all_to_all x1 -> x0, waiting for transfers between devices: 52 us -> none  [shards(): lax.all_to_all(goal_keys, 'goal', split_axis=2, concat_axis=0, tiled=True)]
    all_gather x1, blocking collectives: 44.1 us -> 87.6 us  [shards(): goal_ids = lax.all_gather(tactic_goal[:, 0], 'goal', axis=0, tiled=True)]
    unnamed x2 -> x1, other arithmetic: 44.6 us -> 21.7 us
    all_to_all x1, starting transfers between devices: 4.75 us -> 12.7 us  [shards(): lax.all_to_all(queries, 'goal', split_axis=2, concat_axis=0, tiled=True)]
    ppermute x0 -> x15, waiting for transfers between devices: none -> 7.69 us  [sent_to_each(): lax.ppermute(sent, axis, [(d, (d + far) % ways) for d in range(ways)])]
    unnamed x22 -> x57, local copies, waits for them, and re-layouts: 75.4 us -> 77.3 us
  transfers between devices with their start and end apart: 5 -> 19, of which waited for: 3 -> 7; matrix products, arithmetic and copies ran while one was open for 51% -> 49% of each run, Pallas kernels for 0% -> 0%
where the time goes in v1:
time: 490 us; the launch traced here: 488 us
  local copies, waits for them, and re-layouts  133 us (27%)
  blocking collectives  87.6 us (18%)
  starting transfers between devices  81.2 us (17%)
  matrix products  65.4 us (13%)
  waiting for transfers between devices  55.7 us (11%)
  other arithmetic  50.5 us (10%)
  between operations  14.1 us (3%)
    all_gather x1, blocking collectives, shards(): goal_ids = lax.all_gather(tactic_goal[:, 0], 'goal', axis=0, tiled=True)  87.6 us
    unnamed x57, local copies, waits for them, and re-layouts  77.3 us
    ppermute x15, starting transfers between devices, sent_to_each(): lax.ppermute(sent, axis, [(d, (d + far) % ways) for d in range(ways)])  55.8 us
    all_to_all x1, waiting for transfers between devices, shards(): lax.all_to_all(attended, 'goal', split_axis=0, concat_axis=2, tiled=True)  47.3 us
    dot_general x1, matrix products, attend_block(): jnp.einsum('thij,tjhd->tihd', weights, vals_tact, preferred_element_type=...  43.3 us
    unnamed x1, other arithmetic  21.7 us
    sub x1, other arithmetic, attend_block(): powers = jnp.exp(scores - biggest)  14.8 us
    dot_general x1, matrix products, attend_block(): jnp.einsum('tihd,tjhd->thij', query_four, keys_tact, preferred_element_ty...  12.7 us
  transfers between devices with their start and end apart: 19, of which 7 were waited for; matrix products, arithmetic and copies ran while one was open for 49% of the time, Pallas kernels for 0%

profile of v1, /device:TPU:13, one launch (start us, length us, event | category | flops | bytes accessed | tf_op | source)
XLA Modules:
  0.0 487.6 jit_solution(9663848386074978342)
XLA Ops:
  6.5 0.7 all-gather.3.cloned.1.call-update
  7.3 10.0 %copy.20 = bf16[1,256,4096]{1,0,2:T(2,128)(2,1)} copy(bf16[1,256,4096]{2,1,0:T(8,128)(2,1)} %param.10) | data formatting | bytes 4194304 | tf_op args[2]
  17.8 21.7 %reduce = bf16[4096,256]{1,0:T(8,128)(2,1)S(1)} reduce(bf16[4096,1,256]{2,1,0:T(2,128)(2,1)} %bitcast.51, bf16[]{:T(256)} %broadcast.34), dimensions={1}, to_apply=%bitcast.40.reduce_sub_computation | reduce | bytes 4194306
  39.5 2.1 reshape.91
  41.5 6.6 %all-to-all-start = ((bf16[16,2,32768]{2,1,0:T(2,128)(2,1)}), bf16[16,2,32768]{2,1,0:T(2,128)(2,1)}, u32[]{:S(2)}, u32[]{:S(2)}) async-start(bf16[16,2,32768]{2,1,0:T(2,128)(2,1)} %reshape.91), calls=%async_computation | async-start | bytes 4194304 | tf_op jit(solution)/shard_map/all_to_all | solution.py:60
  48.1 2.3 fusion.9
  50.5 1.0 fusion.19
  52.1 1.5 collective-permute-start.2
  53.6 3.2 collective-permute-start.3
  58.3 87.6 %all-reduce = s32[64]{0:T(128)S(1)} all-reduce(s32[64]{0:T(128)S(1)} %bitcast_dynamic-update-slice_fusion), channel_id=2, replica_groups=mesh['groups'=2,'goal'=16] {'goal'}, use_global_device_ids=true, to_apply=%add | all-reduce | flops 64 | bytes 512 | tf_op jit(solution)/shard_map/all_gather | solution.py:57
  146.0 6.9 %copy.24 = bf16[4,64,4096]{1,0,2:T(4,128)(2,1)} copy(bf16[4,64,4096]{2,1,0:T(8,128)(2,1)} %param.8) | data formatting | bytes 4194304 | tf_op args[0]
  152.9 7.6 %reshape.93 = bf16[16,2,32768]{2,1,0:T(2,128)(2,1)} reshape(bf16[4096,4,64]{2,1,0:T(4,128)(2,1)} %bitcast.54) | data formatting | bytes 4194304
  160.5 29.4 %collective-permute-start.5 = (bf16[1,256,256]{2,1,0:T(8,128)(2,1)S(1)}, bf16[1,256,256]{2,1,0:T(8,128)(2,1)S(1)}, u32[]{:S(2)}, u32[]{:S(2)}) collective-permute-start(bf16[1,256,256]{2,1,0:T(8,128)(2,1)S(1)} %get-tuple-element.33), channel_id=1, source_target_pairs={{0,10},{1,11},{2,12},{3,13},{4,14},{5,15},{6,0},{7,1},{8,2},{9,3},... | collective-permute-start | bytes 393224 | tf_op jit(solution)/shard_map/ppermute | solution.py:17
  190.6 10.9 %collective-permute-start.6 = (bf16[1,256,256]{2,1,0:T(8,128)(2,1)}, bf16[1,256,256]{2,1,0:T(8,128)(2,1)S(1)}, u32[]{:S(2)}, u32[]{:S(2)}) collective-permute-start(bf16[1,256,256]{2,1,0:T(8,128)(2,1)} %get-tuple-element.32), channel_id=1, source_target_pairs={{0,9},{1,10},{2,11},{3,12},{4,13},{5,14},{6,15},{7,0},{8,1},{9,2},... | collective-permute-start | bytes 393224 | tf_op jit(solution)/shard_map/ppermute | solution.py:17
  202.8 2.9 collective-permute-start.8
  208.4 4.1 collective-permute-start.11
  213.8 1.5 collective-permute-start.13
  216.4 0.8 collective-permute-start.14
  217.9 1.4 collective-permute-done.10
  219.9 2.1 collective-permute-done.11
  223.4 1.5 collective-permute-done.12
  226.2 1.5 collective-permute-done.13
  231.7 12.7 %all-to-all-start.1 = ((bf16[16,2,32768]{2,1,0:T(2,128)(2,1)}), bf16[16,2,32768]{2,1,0:T(2,128)(2,1)}, u32[]{:S(2)}, u32[]{:S(2)}) async-start(bf16[16,2,32768]{2,1,0:T(2,128)(2,1)} %reshape.93), calls=%async_computation.1 | async-start | bytes 4194304 | tf_op jit(solution)/shard_map/all_to_all | solution.py:62
  251.7 1.6 constant_dynamic-update-slice_fusion.3
  253.3 1.6 constant_dynamic-update-slice_fusion.2
  254.8 1.6 constant_dynamic-update-slice_fusion.1
  256.4 1.6 constant_dynamic-update-slice_fusion
  258.6 1.7 constant_dynamic-slice_fusion
  260.3 5.5 %gather_fusion.1 = bf16[64,256,256]{2,1,0:T(8,128)(2,1)} fusion(bf16[16,256,256]{2,1,0:T(8,128)(2,1)S(1)} %constant_dynamic-slice_fusion, s32[1024]{0:T(1024)S(1)} %pad_clamp_fusion), kind=kCustom, calls=%fused_computation.1.clone | custom fusion | bytes 16777472 | tf_op jit(solution)/shard_map/while/body/eval_jaxpr/jit(_take)/gather | solution.py:27
  265.9 10.5 %reshape.92 = bf16[4096,1,256]{2,1,0:T(2,128)(2,1)} reshape(bf16[16,2,32768]{2,1,0:T(2,128)(2,1)} %all-to-all-done) | data formatting | bytes 4194304
  276.3 3.9 copy.29
  280.2 2.8 copy.21
  283.1 5.5 %gather_fusion = bf16[64,256,256]{2,1,0:T(8,128)(2,1)} fusion(bf16[16,256,256]{2,1,0:T(8,128)(2,1)S(1)} %bitcast.50, s32[1024]{0:T(1024)S(1)} %pad_clamp_fusion), kind=kCustom, calls=%fused_computation.clone | custom fusion | bytes 16777472 | tf_op jit(solution)/shard_map/while/body/eval_jaxpr/jit(_take)/gather | solution.py:28
  288.6 11.6 %broadcast_select_fusion = (bf16[64,256,256]{2,1,0:T(8,128)(2,1)}, bf16[64,256,256]{2,1,0:T(8,128)(2,1)}) fusion(bf16[64,256,256]{2,1,0:T(8,128)(2,1)} %gather_fusion.1, pred[64]{0:T(512)(128)(4,1)S(1)} %compare_and_fusion, bf16[64,256,256]{2,1,0:T(8,128)(2,1)} %gather_fusion), kind=kLoop, calls=%fused_computation.9 | loop fusion | flops 8388608 | bytes 33554496 | tf_op jit(solution)/shard_map/while/body/eval_jaxpr/jit(_take)/select_n | solution.py:27
  300.2 12.0 %copy.23 = bf16[64,256,256]{1,2,0:T(8,128)(2,1)} copy(bf16[64,256,256]{2,1,0:T(8,128)(2,1)} %get-tuple-element.39) | data formatting | bytes 16777216 | tf_op jit(solution)/shard_map/while/body/eval_jaxpr/jit(_take)/select_n | solution.py:27
  312.2 7.4 %reshape.94 = bf16[4096,4,64]{2,1,0:T(4,128)(2,1)} reshape(bf16[16,2,32768]{2,1,0:T(2,128)(2,1)} %all-to-all-done.1) | data formatting | bytes 4194304
  319.6 5.4 %copy.25 = bf16[4,64,16,256]{3,1,0,2:T(8,128)(2,1)S(1)} copy(bf16[4,64,16,256]{1,0,3,2:T(4,128)(2,1)} %bitcast.53) | data formatting | bytes 4194304 | tf_op jit(solution)/shard_map/all_to_all | solution.py:62
  325.0 3.3 reshape.60
  328.2 11.9 %copy.22 = bf16[64,256,256]{1,2,0:T(8,128)(2,1)} copy(bf16[64,256,256]{2,1,0:T(8,128)(2,1)} %get-tuple-element.40) | data formatting | bytes 16777216 | tf_op jit(solution)/shard_map/while/body/eval_jaxpr/jit(_take)/select_n | solution.py:28
  340.2 12.7 %fusion.6 = f32[64,4,256,64]{2,3,1,0:T(8,128)} fusion(bf16[64,256,4,64]{1,3,2,0:T(8,128)(2,1)} %bitcast.49, bf16[64,64,4,64]{3,2,1,0:T(4,128)(2,1)} %reshape.60), kind=kOutput, calls=%fused_computation.13 | convolution fusion | flops 536870912 | bytes 27262976 | tf_op jit(solution)/shard_map/while/body/eval_jaxpr/tihd,tjhd->thij/dot_general | solution.py:30
  352.9 14.8 %fusion.20 = f32[64,4,64]{2,1,0:T(4,128)S(1)} fusion(f32[64,4,256,64]{2,3,1,0:T(8,128)} %fusion.6), kind=kOutput, calls=%fused_computation.62 | output fusion | flops 8388863 | bytes 16842752 | tf_op jit(solution)/shard_map/while/body/eval_jaxpr/sub | solution.py:34
  367.7 43.3 %fusion.8 = bf16[64,4,64,64]{3,2,1,0:T(8,128)(2,1)} fusion(bf16[64,256,4,64]{1,3,2,0:T(8,128)(2,1)} %bitcast.57, f32[64,4,64]{2,1,0:T(4,128)S(1)} %fusion.20, f32[64,4,256,64]{2,3,1,0:T(8,128)} %fusion.6), kind=kOutput, calls=%fused_computation.15 | convolution fusion | flops 550519040 | bytes 27328512 | tf_op jit(solution)/shard_map/while/body/eval_jaxpr/thij,tjhd->tihd/dot_general | solution.py:36
  411.0 4.8 copy.27
  415.8 6.1 %all-to-all-start.2 = ((bf16[64,64,256]{2,1,0:T(8,128)(2,1)}), bf16[64,64,256]{2,1,0:T(8,128)(2,1)S(1)}, u32[]{:S(2)}, u32[]{:S(2)}) async-start(bf16[64,64,256]{2,1,0:T(8,128)(2,1)} %copy.27), calls=%async_computation.2 | async-start | bytes 4194304 | tf_op jit(solution)/shard_map/all_to_all | solution.py:64
  422.1 47.3 %all-to-all-done.2 = bf16[64,64,256]{2,1,0:T(8,128)(2,1)S(1)} async-done(((bf16[64,64,256]{2,1,0:T(8,128)(2,1)}), bf16[64,64,256]{2,1,0:T(8,128)(2,1)S(1)}, u32[]{:S(2)}, u32[]{:S(2)}) %all-to-all-start.2) | async-done | bytes 2097184 | tf_op jit(solution)/shard_map/all_to_all | solution.py:64
  469.3 1.2 copy.28
  470.5 0.9 copy.30
  471.5 9.3 %convolution_convert_fusion = bf16[256,2048]{1,0:T(8,128)(2,1)} fusion(bf16[4096,2048]{1,0:T(8,128)(2,1)} %all-gather.3.cloned.1.call-done, bf16[256,4096]{1,0:T(8,128)(2,1)S(1)} %bitcast.61, pred[256]{0:T(512)(128)(4,1)S(1)} %lt.52), kind=kOutput, calls=%fused_computation.16 | convolution fusion | flops 4296540160 | bytes 19923200 | tf_op jit(solution)/shard_map/dot_general | solution.py:70
  (73 shorter events, 25.2 us)
Async XLA Ops:
  6.5 464.9 %all-gather.3.cloned.1.call-start = ((), (), s32[]{:S(2)}) async-start(), calls=%async_computation.3 | async-start | bytes 17825792 | tf_op jit(solution)/shard_map/all_gather | solution.py:72
  41.5 190.1 %all-to-all-start = ((bf16[16,2,32768]{2,1,0:T(2,128)(2,1)}), bf16[16,2,32768]{2,1,0:T(2,128)(2,1)}, u32[]{:S(2)}, u32[]{:S(2)}) async-start(bf16[16,2,32768]{2,1,0:T(2,128)(2,1)} %reshape.91), calls=%async_computation | async-start | bytes 4194304 | tf_op jit(solution)/shard_map/all_to_all | solution.py:60
  48.1 9.0 %copy-start.6 = (u32[32]{0:T(128)S(1)}, u32[32]{0:T(128)}, u32[]{:S(2)}) copy-start(u32[32]{0:T(128)} %constant.86) | copy-start | bytes 388
  48.1 10.1 %copy-start.4 = (s32[4,1]{0,1:T(1,128)S(1)}, s32[4,1]{0,1:T(1,128)}, u32[]{:S(2)}) copy-start(s32[4,1]{0,1:T(1,128)} %param.12) | copy-start | bytes 52
  51.5 109.0 %collective-permute-start = (bf16[1,256,256]{2,1,0:T(8,128)(2,1)S(1)}, bf16[1,256,256]{2,1,0:T(8,128)(2,1)S(1)}, u32[]{:S(2)}, u32[]{:S(2)}) collective-permute-start(bf16[1,256,256]{2,1,0:T(8,128)(2,1)S(1)} %get-tuple-element.38), channel_id=1, source_target_pairs={{0,15},{1,0},{2,1},{3,2},{4,3},{5,4},{6,5},{7,6},{8,7},{9,8},{10,9... | collective-permute-start | bytes 393224 | tf_op jit(solution)/shard_map/ppermute | solution.py:17
  51.8 138.8 %collective-permute-start.1 = (bf16[1,256,256]{2,1,0:T(8,128)(2,1)S(1)}, bf16[1,256,256]{2,1,0:T(8,128)(2,1)S(1)}, u32[]{:S(2)}, u32[]{:S(2)}) collective-permute-start(bf16[1,256,256]{2,1,0:T(8,128)(2,1)S(1)} %get-tuple-element.37), channel_id=1, source_target_pairs={{0,14},{1,15},{2,0},{3,1},{4,2},{5,3},{6,4},{7,5},{8,6},{9,7},{10,... | collective-permute-start | bytes 393224 | tf_op jit(solution)/shard_map/ppermute | solution.py:17
  52.1 150.1 %collective-permute-start.2 = (bf16[1,256,256]{2,1,0:T(8,128)(2,1)S(1)}, bf16[1,256,256]{2,1,0:T(8,128)(2,1)S(1)}, u32[]{:S(2)}, u32[]{:S(2)}) collective-permute-start(bf16[1,256,256]{2,1,0:T(8,128)(2,1)S(1)} %get-tuple-element.36), channel_id=1, source_target_pairs={{0,13},{1,14},{2,15},{3,0},{4,1},{5,2},{6,3},{7,4},{8,5},{9,6},{10... | collective-permute-start | bytes 393224 | tf_op jit(solution)/shard_map/ppermute | solution.py:17
  53.6 149.2 %collective-permute-start.3 = (bf16[1,256,256]{2,1,0:T(8,128)(2,1)S(1)}, bf16[1,256,256]{2,1,0:T(8,128)(2,1)S(1)}, u32[]{:S(2)}, u32[]{:S(2)}) collective-permute-start(bf16[1,256,256]{2,1,0:T(8,128)(2,1)S(1)} %get-tuple-element.35), channel_id=1, source_target_pairs={{0,12},{1,13},{2,14},{3,15},{4,0},{5,1},{6,2},{7,3},{8,4},{9,5},{1... | collective-permute-start | bytes 393224 | tf_op jit(solution)/shard_map/ppermute | solution.py:17
  56.8 149.6 %collective-permute-start.4 = (bf16[1,256,256]{2,1,0:T(8,128)(2,1)S(1)}, bf16[1,256,256]{2,1,0:T(8,128)(2,1)S(1)}, u32[]{:S(2)}, u32[]{:S(2)}) collective-permute-start(bf16[1,256,256]{2,1,0:T(8,128)(2,1)S(1)} %get-tuple-element.34), channel_id=1, source_target_pairs={{0,11},{1,12},{2,13},{3,14},{4,15},{5,0},{6,1},{7,2},{8,3},{9,4},{... | collective-permute-start | bytes 393224 | tf_op jit(solution)/shard_map/ppermute | solution.py:17
  160.5 47.2 %collective-permute-start.5 = (bf16[1,256,256]{2,1,0:T(8,128)(2,1)S(1)}, bf16[1,256,256]{2,1,0:T(8,128)(2,1)S(1)}, u32[]{:S(2)}, u32[]{:S(2)}) collective-permute-start(bf16[1,256,256]{2,1,0:T(8,128)(2,1)S(1)} %get-tuple-element.33), channel_id=1, source_target_pairs={{0,10},{1,11},{2,12},{3,13},{4,14},{5,15},{6,0},{7,1},{8,2},{9,3},... | collective-permute-start | bytes 393224 | tf_op jit(solution)/shard_map/ppermute | solution.py:17
  190.6 17.8 %collective-permute-start.6 = (bf16[1,256,256]{2,1,0:T(8,128)(2,1)}, bf16[1,256,256]{2,1,0:T(8,128)(2,1)S(1)}, u32[]{:S(2)}, u32[]{:S(2)}) collective-permute-start(bf16[1,256,256]{2,1,0:T(8,128)(2,1)} %get-tuple-element.32), channel_id=1, source_target_pairs={{0,9},{1,10},{2,11},{3,12},{4,13},{5,14},{6,15},{7,0},{8,1},{9,2},... | collective-permute-start | bytes 393224 | tf_op jit(solution)/shard_map/ppermute | solution.py:17
  202.2 11.0 %collective-permute-start.7 = (bf16[1,256,256]{2,1,0:T(8,128)(2,1)}, bf16[1,256,256]{2,1,0:T(8,128)(2,1)S(1)}, u32[]{:S(2)}, u32[]{:S(2)}) collective-permute-start(bf16[1,256,256]{2,1,0:T(8,128)(2,1)} %get-tuple-element.31), channel_id=1, source_target_pairs={{0,8},{1,9},{2,10},{3,11},{4,12},{5,13},{6,14},{7,15},{8,0},{9,1},... | collective-permute-start | bytes 393224 | tf_op jit(solution)/shard_map/ppermute | solution.py:17
  202.8 11.0 %collective-permute-start.8 = (bf16[1,256,256]{2,1,0:T(8,128)(2,1)}, bf16[1,256,256]{2,1,0:T(8,128)(2,1)S(1)}, u32[]{:S(2)}, u32[]{:S(2)}) collective-permute-start(bf16[1,256,256]{2,1,0:T(8,128)(2,1)} %get-tuple-element.30), channel_id=1, source_target_pairs={{0,7},{1,8},{2,9},{3,10},{4,11},{5,12},{6,13},{7,14},{8,15},{9,0},... | collective-permute-start | bytes 393224 | tf_op jit(solution)/shard_map/ppermute | solution.py:17
  206.4 10.0 %collective-permute-start.9 = (bf16[1,256,256]{2,1,0:T(8,128)(2,1)}, bf16[1,256,256]{2,1,0:T(8,128)(2,1)S(1)}, u32[]{:S(2)}, u32[]{:S(2)}) collective-permute-start(bf16[1,256,256]{2,1,0:T(8,128)(2,1)} %get-tuple-element.29), channel_id=1, source_target_pairs={{0,6},{1,7},{2,8},{3,9},{4,10},{5,11},{6,12},{7,13},{8,14},{9,15},... | collective-permute-start | bytes 393224 | tf_op jit(solution)/shard_map/ppermute | solution.py:17
  207.7 11.6 %collective-permute-start.10 = (bf16[1,256,256]{2,1,0:T(8,128)(2,1)}, bf16[1,256,256]{2,1,0:T(8,128)(2,1)S(1)}, u32[]{:S(2)}, u32[]{:S(2)}) collective-permute-start(bf16[1,256,256]{2,1,0:T(8,128)(2,1)} %get-tuple-element.28), channel_id=1, source_target_pairs={{0,5},{1,6},{2,7},{3,8},{4,9},{5,10},{6,11},{7,12},{8,13},{9,14},{... | collective-permute-start | bytes 393224 | tf_op jit(solution)/shard_map/ppermute | solution.py:17
  208.4 13.7 %collective-permute-start.11 = (bf16[1,256,256]{2,1,0:T(8,128)(2,1)}, bf16[1,256,256]{2,1,0:T(8,128)(2,1)S(1)}, u32[]{:S(2)}, u32[]{:S(2)}) collective-permute-start(bf16[1,256,256]{2,1,0:T(8,128)(2,1)} %get-tuple-element.26), channel_id=1, source_target_pairs={{0,4},{1,5},{2,6},{3,7},{4,8},{5,9},{6,10},{7,11},{8,12},{9,13},{1... | collective-permute-start | bytes 393224 | tf_op jit(solution)/shard_map/ppermute | solution.py:17
  213.1 11.8 %collective-permute-start.12 = (bf16[1,256,256]{2,1,0:T(8,128)(2,1)}, bf16[1,256,256]{2,1,0:T(8,128)(2,1)S(1)}, u32[]{:S(2)}, u32[]{:S(2)}) collective-permute-start(bf16[1,256,256]{2,1,0:T(8,128)(2,1)} %get-tuple-element.24), channel_id=1, source_target_pairs={{0,3},{1,4},{2,5},{3,6},{4,7},{5,8},{6,9},{7,10},{8,11},{9,12},{10... | collective-permute-start | bytes 393224 | tf_op jit(solution)/shard_map/ppermute | solution.py:17
  213.8 13.9 %collective-permute-start.13 = (bf16[1,256,256]{2,1,0:T(8,128)(2,1)}, bf16[1,256,256]{2,1,0:T(8,128)(2,1)S(1)}, u32[]{:S(2)}, u32[]{:S(2)}) collective-permute-start(bf16[1,256,256]{2,1,0:T(8,128)(2,1)} %get-tuple-element.17), channel_id=1, source_target_pairs={{0,2},{1,3},{2,4},{3,5},{4,6},{5,7},{6,8},{7,9},{8,10},{9,11},{10,... | collective-permute-start | bytes 393224 | tf_op jit(solution)/shard_map/ppermute | solution.py:17
  216.4 13.2 %collective-permute-start.14 = (bf16[1,256,256]{2,1,0:T(8,128)(2,1)}, bf16[1,256,256]{2,1,0:T(8,128)(2,1)S(1)}, u32[]{:S(2)}, u32[]{:S(2)}) collective-permute-start(bf16[1,256,256]{2,1,0:T(8,128)(2,1)} %get-tuple-element.16), channel_id=1, source_target_pairs={{0,1},{1,2},{2,3},{3,4},{4,5},{5,6},{6,7},{7,8},{8,9},{9,10},{10,1... | collective-permute-start | bytes 393224 | tf_op jit(solution)/shard_map/ppermute | solution.py:17
  222.1 0.6 copy-start
  224.9 0.7 copy-start.1
  227.7 0.7 copy-start.2
  229.7 0.7 copy-start.3
  231.7 80.5 %all-to-all-start.1 = ((bf16[16,2,32768]{2,1,0:T(2,128)(2,1)}), bf16[16,2,32768]{2,1,0:T(2,128)(2,1)}, u32[]{:S(2)}, u32[]{:S(2)}) async-start(bf16[16,2,32768]{2,1,0:T(2,128)(2,1)} %reshape.93), calls=%async_computation.1 | async-start | bytes 4194304 | tf_op jit(solution)/shard_map/all_to_all | solution.py:62
  411.0 10.9 %copy-start.5 = (s32[4]{0:T(128)S(1)}, s32[4]{0:T(128)}, u32[]{:S(2)}) copy-start(s32[4]{0:T(128)} %param.13) | copy-start | bytes 52
  415.8 53.5 %all-to-all-start.2 = ((bf16[64,64,256]{2,1,0:T(8,128)(2,1)}), bf16[64,64,256]{2,1,0:T(8,128)(2,1)S(1)}, u32[]{:S(2)}, u32[]{:S(2)}) async-start(bf16[64,64,256]{2,1,0:T(8,128)(2,1)} %copy.27), calls=%async_computation.2 | async-start | bytes 4194304 | tf_op jit(solution)/shard_map/all_to_all | solution.py:64
Sparse Core Ops, SparseCore 0:
  9.5 166.1 all-gather.2
